TPU v7x, 512 devices: a whole 4x8x8 slice. The times are simulated.
512 devices in a mesh: pipe: 8 (over y), seq: 8 (over x, core), dp: 8 (over z).
Axes of the slice: x: 4, y: 8, z: 8, core: 2. Of those that a mesh axis runs over, the one named last changes fastest.
Arguments:
- incoming: bfloat16 [8, 3, 8, 1024, 1536], P('pipe', None, 'dp', 'seq'), may hold values from -9 to 9, as said below
- contacts: int32 [10, 8, 1024], P(None, 'dp', 'seq'), may hold values from 0 to 15
- keyframes: int32 [10, 8, 1024], P(None, 'dp'), may hold values 0 or 1
- timesteps: int32 [10, 8], P(None, 'dp'), may hold values from 0 to 999
- w_query: bfloat16 [8, 1536, 1536], P('pipe', ('seq', 'dp')), may hold values from -1 to 1, as said below
- w_keyval: bfloat16 [8, 1536, 1536], P('pipe', ('seq', 'dp')), may hold values from -1 to 1, as said below
- norm_gain: float32 [8, 1536], P('pipe'), may hold values from 0.5 to 1.5
- time_freq: float32 [8, 1536], P('pipe'), may hold values from 0.0005 to 0.05
- contact_table: bfloat16 [8, 16, 1536], P('pipe'), may hold values from -3 to 3
- key_bias: float32 [8, 16], P('pipe'), may hold values from 0.5 to 4
- attn_gate: float32 [8, 1536], P('pipe'), may hold values from 1 to 4
- head_cotangent: bfloat16 [8, 3, 8, 1024, 256], P('pipe', None, 'dp', 'seq'), may hold values from -6 to 6
Outputs:
- section_out: bfloat16 [8, 3, 8, 1024, 1536], P('pipe', None, 'dp', 'seq')
- head_grad: float32 [8, 1536, 256], P('pipe', ('seq', 'dp'))
Inputs may be any that keep to these rules, and one draw needn't show every extreme that they name: `contacts`: each frame's contact state, four limbs as bits. `incoming`: activations of order one. `w_query`: entries of about 1536 ** -0.5. `w_keyval`: entries of about 1536 ** -0.5.
All inputs are finite; a program needn't handle non-finite values. No bound on the sum of `keyframes` on one device may be relied on, other than what follows from the above.
Results may differ from a plain program's by a relative error of at most 0.014.
Values may be sent and summed in bfloat16 or wider, within the bound.
A program may use at most 64 MiB of HBM per device.

v0:
```python
import jax
import jax.numpy as jnp
from jax import lax
from jax.sharding import PartitionSpec as P

epsilon = 1e-06


def passed_along(value, axis, steps):
    count = lax.axis_size(axis)
    first, last = (max(0, -steps), min(count, count - steps))
    return lax.ppermute(value, axis, [(source, source + steps) for source in range(first, last)])


def body(
    incoming,
    contacts,
    keyframes,
    timesteps,
    w_query,
    w_keyval,
    norm_gain,
    time_freq,
    contact_table,
    key_bias,
    attn_gate,
    head_cotangent,
):
    section_idx = lax.axis_index("pipe")
    seq_idx = lax.axis_index("seq")
    seq_count = lax.axis_size("seq")
    section_count = lax.axis_size("pipe")
    rep_count = lax.axis_size("dp")
    tok_rows = incoming.shape[3]
    width = incoming.shape[4]
    turns = incoming.shape[1]
    frames = tok_rows * seq_count
    heads_all = key_bias.shape[1]
    head_size = width // heads_all
    heads_local = heads_all // seq_count
    kv_width = w_keyval.shape[2]
    kv_local = kv_width // (2 * head_size * seq_count)
    group_size = heads_local // kv_local
    feat_count = head_cotangent.shape[4]
    score_scale = head_size ** (-0.5)
    gathered = (
        lax.all_gather(w_query, ("seq", "dp"), axis=1, tiled=True),
        lax.all_gather(w_keyval, ("seq", "dp"), axis=1, tiled=True),
    )
    wquery = gathered[0][0]
    wkeyval = gathered[1][0]
    gain_row = norm_gain[0]
    freq_row = time_freq[0]
    table = contact_table[0]
    gate_row = attn_gate[0]
    bias_local = lax.dynamic_slice_in_dim(key_bias[0], seq_idx * heads_local, heads_local)
    contact_all = contacts[:, 0, :]
    key_all = keyframes[:, 0, :]
    step_all = timesteps[:, 0]
    labels = jnp.arange(table.shape[0], dtype=jnp.int32)
    outputs = []
    handed = None
    for turn in range(turns):
        fresh_rows = incoming[0, turn, 0]
        if turn == 0:
            current = fresh_rows
        else:
            current = jnp.where(section_idx == 0, fresh_rows, handed)
        batch_idx = turn - section_idx + section_count - 1
        contact_rows = lax.dynamic_index_in_dim(contact_all, batch_idx, 0, keepdims=False)
        key_flags = lax.dynamic_index_in_dim(key_all, batch_idx, 0, keepdims=False).astype(
            jnp.float32
        )
        timestep = lax.dynamic_index_in_dim(step_all, batch_idx, 0, keepdims=False).astype(
            jnp.float32
        )
        onehot = (contact_rows[:, None] == labels[None, :]).astype(jnp.bfloat16)
        embedded = jnp.dot(onehot, table, preferred_element_type=jnp.float32)
        hidden = current.astype(jnp.float32) + embedded
        root_mean = jnp.sqrt(jnp.mean(hidden * hidden, axis=-1, keepdims=True) + epsilon)
        modulation = gain_row * (1.0 + 0.5 * jnp.sin(timestep * freq_row))
        normed = (hidden / root_mean * modulation[None, :]).astype(jnp.bfloat16)
        queries = jnp.dot(normed, wquery, preferred_element_type=jnp.float32).astype(jnp.bfloat16)
        keyval = jnp.dot(normed, wkeyval, preferred_element_type=jnp.float32).astype(jnp.bfloat16)
        query_parts = queries.reshape(tok_rows, seq_count, width // seq_count)
        keyval_parts = keyval.reshape(tok_rows, seq_count, kv_width // seq_count)
        regrouped = (
            lax.all_to_all(query_parts, "seq", split_axis=1, concat_axis=0, tiled=True),
            lax.all_to_all(keyval_parts, "seq", split_axis=1, concat_axis=0, tiled=True),
        )
        query_heads = regrouped[0].reshape(frames, heads_local, head_size)
        keyval_heads = regrouped[1].reshape(frames, kv_local, 2, head_size)
        head_outputs = []
        for head in range(heads_local):
            key_rows = keyval_heads[:, head // group_size, 0]
            value_rows = keyval_heads[:, head // group_size, 1]
            scores = (
                lax.dot_general(
                    query_heads[:, head],
                    key_rows,
                    (((1,), (1,)), ((), ())),
                    preferred_element_type=jnp.float32,
                )
                * score_scale
            )
            scores = scores + bias_local[head] * key_flags[None, :]
            row_max = jnp.max(scores, axis=-1, keepdims=True)
            exponent = jnp.exp(scores - row_max)
            probabilities = (exponent / jnp.sum(exponent, axis=-1, keepdims=True)).astype(
                jnp.bfloat16
            )
            head_outputs.append(
                jnp.dot(probabilities, value_rows, preferred_element_type=jnp.float32).astype(
                    jnp.bfloat16
                )
            )
        attended = jnp.stack(head_outputs, axis=1).reshape(frames, heads_local * head_size)
        returned = lax.all_to_all(attended, "seq", split_axis=0, concat_axis=1, tiled=True)
        output = (hidden + gate_row[None, :] * returned.astype(jnp.float32)).astype(jnp.bfloat16)
        outputs.append(output)
        if turn + 1 < turns:
            handed = passed_along(output, "pipe", 1)
    stacked = jnp.stack(outputs)
    section_out = stacked[None, :, None]
    flat_out = stacked.reshape(turns * tok_rows, width)
    flat_cot = head_cotangent[0, :, 0].reshape(turns * tok_rows, feat_count)
    factor = float(turns * rep_count * frames) ** (-0.5)
    grad_rows = lax.psum_scatter(
        lax.dot_general(
            flat_out, flat_cot, (((0,), (0,)), ((), ())), preferred_element_type=jnp.float32
        )
        * factor,
        ("seq", "dp"),
        scatter_dimension=0,
        tiled=True,
    )
    return (section_out, grad_rows[None])


def solution(mesh):
    in_specs = (
        P("pipe", None, "dp", "seq", None),
        P(None, "dp", "seq"),
        P(None, "dp", None),
        P(None, "dp"),
        P("pipe", ("seq", "dp"), None),
        P("pipe", ("seq", "dp"), None),
        P("pipe", None),
        P("pipe", None),
        P("pipe", None, None),
        P("pipe", None),
        P("pipe", None),
        P("pipe", None, "dp", "seq", None),
    )
    out_specs = (P("pipe", None, "dp", "seq", None), P("pipe", ("seq", "dp"), None))
    return jax.shard_map(body, mesh=mesh, in_specs=in_specs, out_specs=out_specs, check_vma=False)
```

profile of v0, /device:TPU:8, one launch (start us, length us, event | category | flops | bytes accessed | tf_op | source)
XLA Modules:
  0.0 502.9 jit_solution(17415926230523855256)
XLA Ops:
  8.7 1.4 constant_dynamic-slice_fusion.4
  12.7 1.2 multiply_reduce_fusion.3
  14.0 1.4 multiply_reduce_fusion.2
  15.4 86.2 %all-gather.3.cloned.1.call-done = bf16[1,1536,1536]{2,1,0:T(8,128)(2,1)} async-done(((bf16[1,24,1536]{2,1,0:T(8,128)(2,1)}), bf16[1,1536,1536]{2,1,0:T(8,128)(2,1)}) %all-gather.3.cloned.1.call-update) | async-done | bytes 4718608 | tf_op jit(solution)/shard_map/all_gather | solution.py:47
  101.6 3.2 fusion.24
  104.8 0.9 copy.37
  105.7 3.5 all-to-all-start
  109.1 78.3 %all-gather.5.cloned.1.call-done = bf16[1,1536,1536]{2,1,0:T(8,128)(2,1)} async-done(((bf16[1,24,1536]{2,1,0:T(8,128)(2,1)}), bf16[1,1536,1536]{2,1,0:T(8,128)(2,1)}) %all-gather.5.cloned.1.call-update) | async-done | bytes 4718608 | tf_op jit(solution)/shard_map/all_gather | solution.py:48
  187.5 3.2 fusion.33
  190.7 0.9 copy.39
  191.6 3.5 all-to-all-start.1
  195.8 2.0 convert_multiply_fusion.1
  198.2 5.7 %all-to-all-done.1 = bf16[128,8,192]{0,2,1:T(8,128)(2,1)S(1)} async-done(((bf16[128,8,192]{0,2,1:T(8,128)(2,1)}), bf16[128,8,192]{0,2,1:T(8,128)(2,1)S(1)}, u32[]{:S(2)}, u32[]{:S(2)}) %all-to-all-start.1) | async-done | bytes 393248 | tf_op jit(solution)/shard_map/all_to_all | solution.py:89
  206.0 1.2 fusion.54
  208.9 1.2 fusion.55
  211.1 3.5 all-to-all-start.2
  214.6 8.8 %all-to-all-done.2 = bf16[8,128,192]{1,2,0:T(8,128)(2,1)S(1)} async-done(((bf16[8,128,192]{1,2,0:T(8,128)(2,1)}), bf16[8,128,192]{1,2,0:T(8,128)(2,1)S(1)}, u32[]{:S(2)}, u32[]{:S(2)}) %all-to-all-start.2) | async-done | bytes 393248 | tf_op jit(solution)/shard_map/all_to_all | solution.py:118
  223.8 3.4 collective-permute-start
  227.2 9.1 %collective-permute-done = bf16[128,1536]{1,0:T(8,128)(2,1)S(1)} collective-permute-done((bf16[128,1536]{1,0:T(8,128)(2,1)S(1)}, bf16[128,1536]{1,0:T(8,128)(2,1)S(1)}, u32[]{:S(2)}, u32[]{:S(2)}) %collective-permute-start) | collective-permute-done | bytes 393248 | tf_op jit(solution)/shard_map/ppermute | solution.py:12
  236.4 1.4 multiply_reduce_fusion.1
  237.8 3.2 fusion.27
  241.0 0.9 copy.43
  241.9 3.6 all-to-all-start.3
  245.5 3.2 fusion.36
  248.7 0.9 copy.45
  249.6 4.6 all-to-all-done.3
  254.2 3.5 all-to-all-start.4
  258.1 8.4 %all-to-all-done.4 = bf16[128,8,192]{0,2,1:T(8,128)(2,1)S(1)} async-done(((bf16[128,8,192]{0,2,1:T(8,128)(2,1)}), bf16[128,8,192]{0,2,1:T(8,128)(2,1)S(1)}, u32[]{:S(2)}, u32[]{:S(2)}) %all-to-all-start.4) | async-done | bytes 393248 | tf_op jit(solution)/shard_map/all_to_all | solution.py:89
  268.6 1.2 fusion.56
  271.5 1.2 fusion.57
  272.9 11.3 %all_to_all.129 = bf16[8,128,192]{1,2,0:T(8,128)(2,1)S(1)} all-to-all(bf16[8,128,192]{1,2,0:T(8,128)(2,1)S(1)} %copy.47), channel_id=1, replica_groups=mesh['pipe'=8,'seq'=8,'dp'=8] {'seq'}, dimensions={0} | all-to-all | bytes 786432 | tf_op jit(solution)/shard_map/all_to_all | solution.py:118
  284.7 3.4 collective-permute-start.1
  288.4 8.8 %collective-permute-done.1 = bf16[128,1536]{1,0:T(8,128)(2,1)S(1)} collective-permute-done((bf16[128,1536]{1,0:T(8,128)(2,1)S(1)}, bf16[128,1536]{1,0:T(8,128)(2,1)S(1)}, u32[]{:S(2)}, u32[]{:S(2)}) %collective-permute-start.1) | collective-permute-done | bytes 393248 | tf_op jit(solution)/shard_map/ppermute | solution.py:12
  297.2 1.2 multiply_reduce_fusion
  298.5 3.2 fusion.30
  301.7 0.9 copy.49
  302.6 3.5 all-to-all-start.6
  306.1 3.2 fusion.39
  309.2 0.9 copy.51
  310.2 4.8 all-to-all-done.6
  314.9 3.5 all-to-all-start.7
  319.1 8.1 %all-to-all-done.7 = bf16[128,8,192]{0,2,1:T(8,128)(2,1)S(1)} async-done(((bf16[128,8,192]{0,2,1:T(8,128)(2,1)}), bf16[128,8,192]{0,2,1:T(8,128)(2,1)S(1)}, u32[]{:S(2)}, u32[]{:S(2)}) %all-to-all-start.7) | async-done | bytes 393248 | tf_op jit(solution)/shard_map/all_to_all | solution.py:89
  329.4 1.2 fusion.58
  332.2 1.2 fusion.59
  333.6 11.3 %all_to_all.130 = bf16[8,128,192]{1,2,0:T(8,128)(2,1)S(1)} all-to-all(bf16[8,128,192]{1,2,0:T(8,128)(2,1)S(1)} %copy.53), channel_id=1, replica_groups=mesh['pipe'=8,'seq'=8,'dp'=8] {'seq'}, dimensions={0} | all-to-all | bytes 786432 | tf_op jit(solution)/shard_map/all_to_all | solution.py:118
  345.4 1.2 pad_maximum_fusion
  346.5 1.8 convolution_multiply_fusion
  348.3 148.0 %reduce-scatter.4.cloned.1.call-done = f32[24,256]{1,0:T(8,128)} async-done(((f32[1536,256]{1,0:T(8,128)}), f32[24,256]{1,0:T(8,128)}) %reduce-scatter.4.cloned.1.call-update) | async-done | bytes 24592
  (65 shorter events, 18.6 us)
Async XLA Ops:
  7.2 339.4 %copy-start = (bf16[1,3,1,128,256]{4,3,2,1,0:T(8,128)(2,1)S(1)}, bf16[1,3,1,128,256]{4,3,2,1,0:T(8,128)(2,1)}, u32[]{:S(2)}) copy-start(bf16[1,3,1,128,256]{4,3,2,1,0:T(8,128)(2,1)} %param.23) | copy-start | bytes 589828
  7.2 94.4 %all-gather.3.cloned.1.call-start = ((), (), s32[]{:S(2)}) async-start(), calls=%async_computation.10 | async-start | bytes 4792320 | tf_op jit(solution)/shard_map/all_gather | solution.py:47
  7.9 179.6 %all-gather.5.cloned.1.call-start = ((), (), s32[]{:S(2)}) async-start(), calls=%async_computation.11 | async-start | bytes 4792320 | tf_op jit(solution)/shard_map/all_gather | solution.py:48
  105.7 85.9 %all-to-all-start = ((bf16[128,8,192]{0,2,1:T(8,128)(2,1)}), bf16[128,8,192]{0,2,1:T(8,128)(2,1)S(1)}, u32[]{:S(2)}, u32[]{:S(2)}) async-start(bf16[128,8,192]{0,2,1:T(8,128)(2,1)} %bitcast.5), calls=%async_computation | async-start | bytes 786432 | tf_op jit(solution)/shard_map/all_to_all | solution.py:88
  109.1 85.9 %copy-start.3 = (f32[1,16]{1,0:T(1,128)S(1)}, f32[1,16]{1,0:T(1,128)}, u32[]{:S(2)}) copy-start(f32[1,16]{1,0:T(1,128)} %param.21) | copy-start | bytes 196
  191.6 12.3 %all-to-all-start.1 = ((bf16[128,8,192]{0,2,1:T(8,128)(2,1)}), bf16[128,8,192]{0,2,1:T(8,128)(2,1)S(1)}, u32[]{:S(2)}, u32[]{:S(2)}) async-start(bf16[128,8,192]{0,2,1:T(8,128)(2,1)} %bitcast.10), calls=%async_computation.1 | async-start | bytes 786432 | tf_op jit(solution)/shard_map/all_to_all | solution.py:89
  208.9 5.6 %copy-start.2 = (f32[1,1536]{1,0:T(1,128)S(1)}, f32[1,1536]{1,0:T(1,128)}, u32[]{:S(2)}) copy-start(f32[1,1536]{1,0:T(1,128)} %param.22) | copy-start | bytes 18436
  210.1 26.3 %copy-start.1 = (bf16[1,16,1536]{2,1,0:T(8,128)(2,1)S(1)}, bf16[1,16,1536]{2,1,0:T(8,128)(2,1)}, u32[]{:S(2)}) copy-start(bf16[1,16,1536]{2,1,0:T(8,128)(2,1)} %param.20) | copy-start | bytes 147460
  211.1 12.3 %all-to-all-start.2 = ((bf16[8,128,192]{1,2,0:T(8,128)(2,1)}), bf16[8,128,192]{1,2,0:T(8,128)(2,1)S(1)}, u32[]{:S(2)}, u32[]{:S(2)}) async-start(bf16[8,128,192]{1,2,0:T(8,128)(2,1)} %copy.41), calls=%async_computation.2 | async-start | bytes 786432 | tf_op jit(solution)/shard_map/all_to_all | solution.py:118
  223.8 12.6 %collective-permute-start = (bf16[128,1536]{1,0:T(8,128)(2,1)S(1)}, bf16[128,1536]{1,0:T(8,128)(2,1)S(1)}, u32[]{:S(2)}, u32[]{:S(2)}) collective-permute-start(bf16[128,1536]{1,0:T(8,128)(2,1)S(1)} %add_convert_fusion.2), channel_id=1, source_target_pairs={{0,64},{64,128},{128,192},{192,256},{256,320},{320,384},{384,448},... | collective-permute-start | bytes 1179656 | tf_op jit(solution)/shard_map/ppermute | solution.py:12
  241.9 12.3 %all-to-all-start.3 = ((bf16[128,8,192]{0,2,1:T(8,128)(2,1)}), bf16[128,8,192]{0,2,1:T(8,128)(2,1)S(1)}, u32[]{:S(2)}, u32[]{:S(2)}) async-start(bf16[128,8,192]{0,2,1:T(8,128)(2,1)} %bitcast.28), calls=%async_computation.3 | async-start | bytes 786432 | tf_op jit(solution)/shard_map/all_to_all | solution.py:88
  254.2 12.3 %all-to-all-start.4 = ((bf16[128,8,192]{0,2,1:T(8,128)(2,1)}), bf16[128,8,192]{0,2,1:T(8,128)(2,1)S(1)}, u32[]{:S(2)}, u32[]{:S(2)}) async-start(bf16[128,8,192]{0,2,1:T(8,128)(2,1)} %bitcast.32), calls=%async_computation.4 | async-start | bytes 786432 | tf_op jit(solution)/shard_map/all_to_all | solution.py:89
  284.7 12.6 %collective-permute-start.1 = (bf16[128,1536]{1,0:T(8,128)(2,1)S(1)}, bf16[128,1536]{1,0:T(8,128)(2,1)S(1)}, u32[]{:S(2)}, u32[]{:S(2)}) collective-permute-start(bf16[128,1536]{1,0:T(8,128)(2,1)S(1)} %add_convert_fusion.1), channel_id=1, source_target_pairs={{0,64},{64,128},{128,192},{192,256},{256,320},{320,384},{384,448},... | collective-permute-start | bytes 1179656 | tf_op jit(solution)/shard_map/ppermute | solution.py:12
  302.6 12.3 %all-to-all-start.6 = ((bf16[128,8,192]{0,2,1:T(8,128)(2,1)}), bf16[128,8,192]{0,2,1:T(8,128)(2,1)S(1)}, u32[]{:S(2)}, u32[]{:S(2)}) async-start(bf16[128,8,192]{0,2,1:T(8,128)(2,1)} %bitcast.48), calls=%async_computation.6 | async-start | bytes 786432 | tf_op jit(solution)/shard_map/all_to_all | solution.py:88
  314.9 12.3 %all-to-all-start.7 = ((bf16[128,8,192]{0,2,1:T(8,128)(2,1)}), bf16[128,8,192]{0,2,1:T(8,128)(2,1)S(1)}, u32[]{:S(2)}, u32[]{:S(2)}) async-start(bf16[128,8,192]{0,2,1:T(8,128)(2,1)} %bitcast.52), calls=%async_computation.7 | async-start | bytes 786432 | tf_op jit(solution)/shard_map/all_to_all | solution.py:89
  318.4 177.9 %reduce-scatter.4.cloned.1.call-start = ((), (), s32[]{:S(2)}) async-start(), calls=%async_computation.12 | async-start | bytes 1597440
Sparse Core Ops, SparseCore 0:
  11.3 90.1 all-gather.2
  104.9 82.5 all-gather.4
  348.5 147.8 reduce-scatter.3
where the time goes:
time: 504 us; the launch traced here: 503 us
  waiting for transfers between devices  372 us (74%)
  matrix products  35.7 us (7%)
  starting transfers between devices  31.5 us (6%)
  blocking collectives  22.7 us (5%)
  between operations  16.2 us (3%)
  local copies, waits for them, and re-layouts  12.8 us (3%)
  other arithmetic  11.6 us (2%)
    unnamed x4, waiting for transfers between devices  149 us
    all_gather x1, waiting for transfers between devices, body(): lax.all_gather(w_query, ('seq', 'dp'), axis=1, tiled=True)  86.2 us
    all_gather x1, waiting for transfers between devices, body(): lax.all_gather(w_keyval, ('seq', 'dp'), axis=1, tiled=True)  78.3 us
    all_to_all x2, blocking collectives, body(): lax.all_to_all(attended, 'seq', split_axis=0, concat_axis=1, tiled=True)  22.7 us
    all_to_all x3, waiting for transfers between devices, body(): lax.all_to_all(keyval_parts, 'seq', split_axis=1, concat_axis=0, tiled=True)  22.2 us
    ppermute x2, waiting for transfers between devices, passed_along(): lax.ppermute(value, axis, [(source, source + steps) for source in range(f...  18 us
    all_to_all x3, starting transfers between devices, body(): lax.all_to_all(query_parts, 'seq', split_axis=1, concat_axis=0, tiled=True)  10.5 us
    all_to_all x3, starting transfers between devices, body(): lax.all_to_all(keyval_parts, 'seq', split_axis=1, concat_axis=0, tiled=True)  10.4 us
  transfers between devices with their start and end apart: 12, of which 11 were waited for; matrix products, arithmetic and copies ran while one was open for 5% of the time, Pallas kernels for 0%

commit v1 on v0

--- a/solution.py
+++ b/solution.py
@@ -4,6 +4,13 @@
 from jax.sharding import PartitionSpec as P
 
 epsilon = 1e-06
+
+
+def all_by_exchange(x, axis, d):
+    devices = lax.axis_size(axis)
+    parts = jnp.stack([x for _ in range(devices)])
+    parts = lax.all_to_all(parts, axis, split_axis=0, concat_axis=0)
+    return jnp.concatenate(parts, axis=d)
 
 
 def passed_along(value, axis, steps):
@@ -44,7 +51,7 @@
     feat_count = head_cotangent.shape[4]
     score_scale = head_size ** (-0.5)
     gathered = (
-        lax.all_gather(w_query, ("seq", "dp"), axis=1, tiled=True),
+        all_by_exchange(w_query, ("seq", "dp"), 1),
         lax.all_gather(w_keyval, ("seq", "dp"), axis=1, tiled=True),
     )
     wquery = gathered[0][0]

time: 504 us -> 475 us (0.942)
  waiting for transfers between devices: 372 us -> 326 us
  starting transfers between devices: 31.5 us -> 46 us
    all_to_all x0 -> x1, waiting for transfers between devices: none -> 113 us  [all_by_exchange(): parts = lax.all_to_all(parts, axis, split_axis=0, concat_axis=0)]
    all_gather x1 -> x0, waiting for transfers between devices: 86.2 us -> none  [body(): lax.all_gather(w_query, ('seq', 'dp'), axis=1, tiled=True)]
    all_gather x1, waiting for transfers between devices: 78.3 us -> 0.02 us  [body(): lax.all_gather(w_keyval, ('seq', 'dp'), axis=1, tiled=True)]
    all_to_all x0 -> x1, starting transfers between devices: none -> 14.2 us  [all_by_exchange(): parts = lax.all_to_all(parts, axis, split_axis=0, concat_axis=0)]
    unnamed x4 -> x3, waiting for transfers between devices: 149 us -> 150 us
where the time goes in v1:
time: 475 us; the launch traced here: 474 us
  waiting for transfers between devices  326 us (69%)
  starting transfers between devices  46 us (10%)
  matrix products  35.9 us (8%)
  blocking collectives  22.7 us (5%)
  between operations  16.5 us (3%)
  local copies, waits for them, and re-layouts  15.5 us (3%)
  other arithmetic  10.9 us (2%)
    unnamed x3, waiting for transfers between devices  150 us
    all_to_all x1, waiting for transfers between devices, all_by_exchange(): parts = lax.all_to_all(parts, axis, split_axis=0, concat_axis=0)  113 us
    all_to_all x2, blocking collectives, body(): lax.all_to_all(attended, 'seq', split_axis=0, concat_axis=1, tiled=True)  22.7 us
    all_to_all x3, waiting for transfers between devices, body(): lax.all_to_all(keyval_parts, 'seq', split_axis=1, concat_axis=0, tiled=True)  22.2 us
    ppermute x2, waiting for transfers between devices, passed_along(): lax.ppermute(value, axis, [(source, source + steps) for source in range(f...  17.6 us
    all_to_all x3, waiting for transfers between devices, body(): lax.all_to_all(query_parts, 'seq', split_axis=1, concat_axis=0, tiled=True)  14.3 us
    all_to_all x1, starting transfers between devices, all_by_exchange(): parts = lax.all_to_all(parts, axis, split_axis=0, concat_axis=0)  14.2 us
    all_to_all x3, starting transfers between devices, body(): lax.all_to_all(query_parts, 'seq', split_axis=1, concat_axis=0, tiled=True)  10.6 us
  transfers between devices with their start and end apart: 12, of which 11 were waited for; matrix products, arithmetic and copies ran while one was open for 5% of the time, Pallas kernels for 0%

profile of v1, /device:TPU:8, one launch (start us, length us, event | category | flops | bytes accessed | tf_op | source)
XLA Modules:
  0.0 473.8 jit_solution(14011235986251828745)
XLA Ops:
  7.2 3.5 stack.28
  10.7 14.2 %all-to-all-start = ((bf16[64,1,24,1536]{3,2,1,0:T(8,128)(2,1)}), bf16[64,1,24,1536]{3,2,1,0:T(8,128)(2,1)}, u32[]{:S(2)}, u32[]{:S(2)}) async-start(bf16[64,1,24,1536]{3,2,1,0:T(8,128)(2,1)} %stack.28), calls=%async_computation | async-start | bytes 9437184 | tf_op jit(solution)/shard_map/all_to_all | solution.py:12
  29.4 1.4 multiply_reduce_fusion.2
  30.8 113.2 %all-to-all-done = bf16[64,1,24,1536]{3,2,1,0:T(8,128)(2,1)} async-done(((bf16[64,1,24,1536]{3,2,1,0:T(8,128)(2,1)}), bf16[64,1,24,1536]{3,2,1,0:T(8,128)(2,1)}, u32[]{:S(2)}, u32[]{:S(2)}) %all-to-all-start) | async-done | bytes 4718624 | tf_op jit(solution)/shard_map/all_to_all | solution.py:12
  144.0 3.2 convolution_convert_fusion.2
  147.2 0.9 copy.37
  148.1 3.7 all-to-all-start.1
  151.8 3.2 fusion.18
  155.0 0.9 copy.39
  155.9 4.8 %all-to-all-done.1 = bf16[128,8,192]{0,2,1:T(8,128)(2,1)S(1)} async-done(((bf16[128,8,192]{0,2,1:T(8,128)(2,1)}), bf16[128,8,192]{0,2,1:T(8,128)(2,1)S(1)}, u32[]{:S(2)}, u32[]{:S(2)}) %all-to-all-start.1) | async-done | bytes 393248 | tf_op jit(solution)/shard_map/all_to_all | solution.py:95
  160.7 3.5 all-to-all-start.2
  164.9 2.0 convert_multiply_fusion.1
  167.4 5.7 %all-to-all-done.2 = bf16[128,8,192]{0,2,1:T(8,128)(2,1)S(1)} async-done(((bf16[128,8,192]{0,2,1:T(8,128)(2,1)}), bf16[128,8,192]{0,2,1:T(8,128)(2,1)S(1)}, u32[]{:S(2)}, u32[]{:S(2)}) %all-to-all-start.2) | async-done | bytes 393248 | tf_op jit(solution)/shard_map/all_to_all | solution.py:96
  175.2 1.2 fusion.39
  178.1 1.2 fusion.40
  180.2 3.5 all-to-all-start.3
  183.7 8.8 %all-to-all-done.3 = bf16[8,128,192]{1,2,0:T(8,128)(2,1)S(1)} async-done(((bf16[8,128,192]{1,2,0:T(8,128)(2,1)}), bf16[8,128,192]{1,2,0:T(8,128)(2,1)S(1)}, u32[]{:S(2)}, u32[]{:S(2)}) %all-to-all-start.3) | async-done | bytes 393248 | tf_op jit(solution)/shard_map/all_to_all | solution.py:125
  193.0 3.7 collective-permute-start
  196.6 8.9 %collective-permute-done = bf16[128,1536]{1,0:T(8,128)(2,1)S(1)} collective-permute-done((bf16[128,1536]{1,0:T(8,128)(2,1)S(1)}, bf16[128,1536]{1,0:T(8,128)(2,1)S(1)}, u32[]{:S(2)}, u32[]{:S(2)}) %collective-permute-start) | collective-permute-done | bytes 393248 | tf_op jit(solution)/shard_map/ppermute | solution.py:19
  205.5 1.4 multiply_reduce_fusion.1
  206.9 3.2 convolution_convert_fusion.1
  210.1 0.9 copy.43
  211.0 3.5 all-to-all-start.4
  214.5 3.2 fusion.21
  217.7 0.9 copy.45
  218.6 4.7 all-to-all-done.4
  223.4 3.5 all-to-all-start.5
  227.3 8.4 %all-to-all-done.5 = bf16[128,8,192]{0,2,1:T(8,128)(2,1)S(1)} async-done(((bf16[128,8,192]{0,2,1:T(8,128)(2,1)}), bf16[128,8,192]{0,2,1:T(8,128)(2,1)S(1)}, u32[]{:S(2)}, u32[]{:S(2)}) %all-to-all-start.5) | async-done | bytes 393248 | tf_op jit(solution)/shard_map/all_to_all | solution.py:96
  237.8 1.2 fusion.41
  240.7 1.2 fusion.42
  242.1 11.3 %all_to_all.134 = bf16[8,128,192]{1,2,0:T(8,128)(2,1)S(1)} all-to-all(bf16[8,128,192]{1,2,0:T(8,128)(2,1)S(1)} %copy.47), channel_id=1, replica_groups=mesh['pipe'=8,'seq'=8,'dp'=8] {'seq'}, dimensions={0} | all-to-all | bytes 786432 | tf_op jit(solution)/shard_map/all_to_all | solution.py:125
  253.9 3.5 collective-permute-start.1
  257.7 8.8 %collective-permute-done.1 = bf16[128,1536]{1,0:T(8,128)(2,1)S(1)} collective-permute-done((bf16[128,1536]{1,0:T(8,128)(2,1)S(1)}, bf16[128,1536]{1,0:T(8,128)(2,1)S(1)}, u32[]{:S(2)}, u32[]{:S(2)}) %collective-permute-start.1) | collective-permute-done | bytes 393248 | tf_op jit(solution)/shard_map/ppermute | solution.py:19
  266.4 1.2 multiply_reduce_fusion
  267.7 3.2 convolution_convert_fusion
  270.9 0.9 copy.49
  271.8 3.5 all-to-all-start.7
  275.3 3.2 fusion.24
  278.5 0.9 copy.51
  279.4 4.7 %all-to-all-done.7 = bf16[128,8,192]{0,2,1:T(8,128)(2,1)S(1)} async-done(((bf16[128,8,192]{0,2,1:T(8,128)(2,1)}), bf16[128,8,192]{0,2,1:T(8,128)(2,1)S(1)}, u32[]{:S(2)}, u32[]{:S(2)}) %all-to-all-start.7) | async-done | bytes 393248 | tf_op jit(solution)/shard_map/all_to_all | solution.py:95
  284.1 3.5 all-to-all-start.8
  288.3 8.1 %all-to-all-done.8 = bf16[128,8,192]{0,2,1:T(8,128)(2,1)S(1)} async-done(((bf16[128,8,192]{0,2,1:T(8,128)(2,1)}), bf16[128,8,192]{0,2,1:T(8,128)(2,1)S(1)}, u32[]{:S(2)}, u32[]{:S(2)}) %all-to-all-start.8) | async-done | bytes 393248 | tf_op jit(solution)/shard_map/all_to_all | solution.py:96
  298.6 1.2 fusion.43
  301.5 1.2 fusion.44
  302.9 11.3 %all_to_all.135 = bf16[8,128,192]{1,2,0:T(8,128)(2,1)S(1)} all-to-all(bf16[8,128,192]{1,2,0:T(8,128)(2,1)S(1)} %copy.53), channel_id=1, replica_groups=mesh['pipe'=8,'seq'=8,'dp'=8] {'seq'}, dimensions={0} | all-to-all | bytes 786432 | tf_op jit(solution)/shard_map/all_to_all | solution.py:125
  314.6 1.2 pad_maximum_fusion
  315.8 1.8 convolution_multiply_fusion
  317.6 149.3 %reduce-scatter.4.cloned.1.call-done = f32[24,256]{1,0:T(8,128)} async-done(((f32[1536,256]{1,0:T(8,128)}), f32[24,256]{1,0:T(8,128)}) %reduce-scatter.4.cloned.1.call-update) | async-done | bytes 24592
  (71 shorter events, 19.1 us)
Async XLA Ops:
  7.2 308.7 %copy-start = (bf16[1,3,1,128,256]{4,3,2,1,0:T(8,128)(2,1)S(1)}, bf16[1,3,1,128,256]{4,3,2,1,0:T(8,128)(2,1)}, u32[]{:S(2)}) copy-start(bf16[1,3,1,128,256]{4,3,2,1,0:T(8,128)(2,1)} %param.23) | copy-start | bytes 589828
  10.6 14.9 %copy-start.5 = (s32[10,1]{0,1:T(1,128)S(1)}, s32[10,1]{0,1:T(1,128)}, u32[]{:S(2)}) copy-start(s32[10,1]{0,1:T(1,128)} %param.15) | copy-start | bytes 124
  10.6 18.2 %copy-start.2 = (f32[1,1536]{1,0:T(1,128)S(1)}, f32[1,1536]{1,0:T(1,128)}, u32[]{:S(2)}) copy-start(f32[1,1536]{1,0:T(1,128)} %param.18) | copy-start | bytes 18436
  10.6 18.2 %copy-start.3 = (f32[1,1536]{1,0:T(1,128)S(1)}, f32[1,1536]{1,0:T(1,128)}, u32[]{:S(2)}) copy-start(f32[1,1536]{1,0:T(1,128)} %param.19) | copy-start | bytes 18436
  10.6 18.7 %copy-start.1 = (bf16[1,16,1536]{2,1,0:T(8,128)(2,1)S(1)}, bf16[1,16,1536]{2,1,0:T(8,128)(2,1)}, u32[]{:S(2)}) copy-start(bf16[1,16,1536]{2,1,0:T(8,128)(2,1)} %param.20) | copy-start | bytes 147460
  10.7 133.4 %all-to-all-start = ((bf16[64,1,24,1536]{3,2,1,0:T(8,128)(2,1)}), bf16[64,1,24,1536]{3,2,1,0:T(8,128)(2,1)}, u32[]{:S(2)}, u32[]{:S(2)}) async-start(bf16[64,1,24,1536]{3,2,1,0:T(8,128)(2,1)} %stack.28), calls=%async_computation | async-start | bytes 9437184 | tf_op jit(solution)/shard_map/all_to_all | solution.py:12
  24.8 127.0 %all-gather.2.cloned.1.call-start = ((), (), s32[]{:S(2)}) async-start(), calls=%async_computation.11 | async-start | bytes 4792320 | tf_op jit(solution)/shard_map/all_gather | solution.py:55
  148.1 12.6 %all-to-all-start.1 = ((bf16[128,8,192]{0,2,1:T(8,128)(2,1)}), bf16[128,8,192]{0,2,1:T(8,128)(2,1)S(1)}, u32[]{:S(2)}, u32[]{:S(2)}) async-start(bf16[128,8,192]{0,2,1:T(8,128)(2,1)} %bitcast.6), calls=%async_computation.1 | async-start | bytes 786432 | tf_op jit(solution)/shard_map/all_to_all | solution.py:95
  151.8 12.4 %copy-start.6 = (f32[1,16]{1,0:T(1,128)S(1)}, f32[1,16]{1,0:T(1,128)}, u32[]{:S(2)}) copy-start(f32[1,16]{1,0:T(1,128)} %param.21) | copy-start | bytes 196
  160.7 12.3 %all-to-all-start.2 = ((bf16[128,8,192]{0,2,1:T(8,128)(2,1)}), bf16[128,8,192]{0,2,1:T(8,128)(2,1)S(1)}, u32[]{:S(2)}, u32[]{:S(2)}) async-start(bf16[128,8,192]{0,2,1:T(8,128)(2,1)} %bitcast.11), calls=%async_computation.2 | async-start | bytes 786432 | tf_op jit(solution)/shard_map/all_to_all | solution.py:96
  178.1 5.6 %copy-start.4 = (f32[1,1536]{1,0:T(1,128)S(1)}, f32[1,1536]{1,0:T(1,128)}, u32[]{:S(2)}) copy-start(f32[1,1536]{1,0:T(1,128)} %param.22) | copy-start | bytes 18436
  180.2 12.3 %all-to-all-start.3 = ((bf16[8,128,192]{1,2,0:T(8,128)(2,1)}), bf16[8,128,192]{1,2,0:T(8,128)(2,1)S(1)}, u32[]{:S(2)}, u32[]{:S(2)}) async-start(bf16[8,128,192]{1,2,0:T(8,128)(2,1)} %copy.41), calls=%async_computation.3 | async-start | bytes 786432 | tf_op jit(solution)/shard_map/all_to_all | solution.py:125
  193.0 12.6 %collective-permute-start = (bf16[128,1536]{1,0:T(8,128)(2,1)S(1)}, bf16[128,1536]{1,0:T(8,128)(2,1)S(1)}, u32[]{:S(2)}, u32[]{:S(2)}) collective-permute-start(bf16[128,1536]{1,0:T(8,128)(2,1)S(1)} %add_convert_fusion.2), channel_id=1, source_target_pairs={{0,64},{64,128},{128,192},{192,256},{256,320},{320,384},{384,448},... | collective-permute-start | bytes 1179656 | tf_op jit(solution)/shard_map/ppermute | solution.py:19
  211.0 12.3 %all-to-all-start.4 = ((bf16[128,8,192]{0,2,1:T(8,128)(2,1)}), bf16[128,8,192]{0,2,1:T(8,128)(2,1)S(1)}, u32[]{:S(2)}, u32[]{:S(2)}) async-start(bf16[128,8,192]{0,2,1:T(8,128)(2,1)} %bitcast.29), calls=%async_computation.4 | async-start | bytes 786432 | tf_op jit(solution)/shard_map/all_to_all | solution.py:95
  223.4 12.3 %all-to-all-start.5 = ((bf16[128,8,192]{0,2,1:T(8,128)(2,1)}), bf16[128,8,192]{0,2,1:T(8,128)(2,1)S(1)}, u32[]{:S(2)}, u32[]{:S(2)}) async-start(bf16[128,8,192]{0,2,1:T(8,128)(2,1)} %bitcast.33), calls=%async_computation.5 | async-start | bytes 786432 | tf_op jit(solution)/shard_map/all_to_all | solution.py:96
  253.9 12.6 %collective-permute-start.1 = (bf16[128,1536]{1,0:T(8,128)(2,1)S(1)}, bf16[128,1536]{1,0:T(8,128)(2,1)S(1)}, u32[]{:S(2)}, u32[]{:S(2)}) collective-permute-start(bf16[128,1536]{1,0:T(8,128)(2,1)S(1)} %add_convert_fusion.1), channel_id=1, source_target_pairs={{0,64},{64,128},{128,192},{192,256},{256,320},{320,384},{384,448},... | collective-permute-start | bytes 1179656 | tf_op jit(solution)/shard_map/ppermute | solution.py:19
  271.8 12.3 %all-to-all-start.7 = ((bf16[128,8,192]{0,2,1:T(8,128)(2,1)}), bf16[128,8,192]{0,2,1:T(8,128)(2,1)S(1)}, u32[]{:S(2)}, u32[]{:S(2)}) async-start(bf16[128,8,192]{0,2,1:T(8,128)(2,1)} %bitcast.49), calls=%async_computation.7 | async-start | bytes 786432 | tf_op jit(solution)/shard_map/all_to_all | solution.py:95
  284.1 12.3 %all-to-all-start.8 = ((bf16[128,8,192]{0,2,1:T(8,128)(2,1)}), bf16[128,8,192]{0,2,1:T(8,128)(2,1)S(1)}, u32[]{:S(2)}, u32[]{:S(2)}) async-start(bf16[128,8,192]{0,2,1:T(8,128)(2,1)} %bitcast.53), calls=%async_computation.8 | async-start | bytes 786432 | tf_op jit(solution)/shard_map/all_to_all | solution.py:96
  287.6 179.4 %reduce-scatter.4.cloned.1.call-start = ((), (), s32[]{:S(2)}) async-start(), calls=%async_computation.12 | async-start | bytes 1597440
Sparse Core Ops, SparseCore 0:
  29.0 114.6 all-gather.1
  317.7 149.1 reduce-scatter.3
